TPU v7x, 512 devices: a whole 4x8x8 slice. The times are simulated.
512 devices in a mesh: branch: 2 (over y_hi), trow: 8 (over z), tcol: 32 (over x, y_lo, core).
Axes of the slice: x: 4, y: 8 (y_hi: 2, y_lo: 4; y = y_hi * 4 + y_lo), z: 8, core: 2. Of those that a mesh axis runs over, the one named last changes fastest.
Arguments:
- latent: bfloat16 [2, 2, 64, 256, 1152], P('branch', None, 'trow', 'tcol'), may hold values from -6 to 6
- modulation: float32 [2, 3, 1152], replicated, may hold values from -2 to 2
- w_query: bfloat16 [2, 1152, 576], P('branch', None, 'tcol'), may hold values from -0.176776695 to 0.176776695
- w_keyval: bfloat16 [2, 1152, 1152], P('branch', None, 'tcol'), may hold values from -3.8301617 to 3.8301617
- w_out: bfloat16 [2, 576, 1152], P('branch', 'tcol'), may hold values from -0.25 to 0.25
- w_zero: bfloat16 [1152, 1152], P(None, 'tcol'), may hold values from -0.1875 to 0.1875
Outputs:
- hidden_out: bfloat16 [2, 2, 64, 256, 1152], P('branch', None, 'trow', 'tcol')
All inputs are finite; a program needn't handle non-finite values.
Results may differ from a plain program's by a relative error of at most 0.0075.
Values may be sent and summed in bfloat16 or wider, within the bound.
A program may use at most 128 MiB of HBM per device.

v0:
```python
import math
import jax
import jax.numpy as jnp
from jax import lax
from jax.sharding import PartitionSpec as P

D = 1152
HD = 72
HEADS = 8
WIN = 13
HW = 576


def padded(block, sides, width):
    for axis, dim in sides:
        count = lax.axis_size(axis)
        forward = [(i, i + 1) for i in range(count - 1)]
        backward = [(target, source) for source, target in forward]
        low = lax.ppermute(
            lax.slice_in_dim(block, block.shape[dim] - width, None, axis=dim), axis, forward
        )
        high = lax.ppermute(lax.slice_in_dim(block, 0, width, axis=dim), axis, backward)
        block = jnp.concatenate([low, block, high], axis=dim)
    return block


def shifted(block, axis, distance):
    devices = range(lax.axis_size(axis))
    route = [(i - distance, i) for i in devices if i - distance in devices]
    return lax.ppermute(block, axis, route)


def modulate(hidden, shift_scale):
    average = jnp.mean(hidden, axis=-1, keepdims=True)
    centred = hidden - average
    variance = jnp.mean(centred * centred, axis=-1, keepdims=True)
    return (centred * lax.rsqrt(variance + 1e-06) * (1.0 + shift_scale[1]) + shift_scale[0]).astype(
        jnp.bfloat16
    )


def block_mask(row_first, col_first, total_rows, total_cols, key_count):
    query_edge = 8
    radius = WIN // 2
    key_side = query_edge + 2 * radius
    offsets = jnp.arange(query_edge)
    reaches = jnp.arange(key_side)
    row_starts = jnp.clip(row_first + offsets - radius, 0, total_rows - WIN)
    key_rows = row_first - radius + reaches
    row_inside = (key_rows[None, :] >= row_starts[:, None]) & (
        key_rows[None, :] < row_starts[:, None] + WIN
    )
    col_starts = jnp.clip(col_first + offsets - radius, 0, total_cols - WIN)
    key_cols = col_first - radius + reaches
    col_inside = (key_cols[None, :] >= col_starts[:, None]) & (
        key_cols[None, :] < col_starts[:, None] + WIN
    )
    joined = row_inside[:, None, :, None] & col_inside[None, :, None, :]
    joined = joined.reshape(query_edge * query_edge, key_side * key_side)
    filler = jnp.zeros((query_edge * query_edge, key_count - key_side * key_side), dtype=jnp.bool_)
    return jnp.concatenate([joined, filler], axis=1)


def edge_keys(key_values):
    radius = WIN // 2
    return padded(key_values, (("trow", 1), ("tcol", 2)), radius)


def attend_tile(queries, extended, row_anchor, col_anchor, total_rows, total_cols):
    images, tile_rows, tile_cols = (queries.shape[0], queries.shape[1], queries.shape[2])
    query_edge = 8
    radius = WIN // 2
    key_side = query_edge + 2 * radius
    key_count = (key_side * key_side + 127) // 128 * 128
    across = tile_cols // query_edge
    block_count = tile_rows // query_edge * across
    scaling = 1.0 / math.sqrt(HD)

    def one_block(position):
        row_block = position // across * query_edge
        col_block = position % across * query_edge
        query_block = queries
        query_block = query_block.reshape(images, query_edge * query_edge, HEADS, HD)
        key_block = extended
        key_block = key_block.reshape(images, key_side * key_side, 2 * HW)
        key_block = jnp.pad(key_block, ((0, 0), (0, key_count - key_side * key_side), (0, 0)))
        key_heads = key_block[..., :HW].reshape(images, key_count, HEADS, HD)
        value_heads = key_block[..., HW:].reshape(images, key_count, HEADS, HD)
        allowed = block_mask(
            row_anchor + row_block, col_anchor + col_block, total_rows, total_cols, key_count
        )
        scores = (
            jnp.einsum(
                "iqhd,ikhd->ihqk", query_block, key_heads, preferred_element_type=jnp.float32
            )
            * scaling
        )
        scores = jnp.where(allowed[None, None], scores, -1e30)
        highest = jnp.max(scores, axis=-1, keepdims=True)
        raised = jnp.exp(scores - highest)
        totals = jnp.sum(raised, axis=-1, keepdims=True)
        weights = (raised / totals).astype(jnp.bfloat16)
        blended = jnp.einsum(
            "ihqk,ikhd->iqhd", weights, value_heads, preferred_element_type=jnp.float32
        )
        return blended.astype(jnp.bfloat16).reshape(images, query_edge, query_edge, HW)

    result = lax.map(one_block, jnp.arange(block_count))
    result = result.reshape(tile_rows // query_edge, across, images, query_edge, query_edge, HW)
    return result.transpose(2, 0, 3, 1, 4, 5).reshape(images, tile_rows, tile_cols, HW)


def run_block(active, hidden, shift_scale, weight_q, weight_kv, weight_o):
    images, tile_rows, tile_cols = (hidden.shape[0], hidden.shape[1], hidden.shape[2])
    tokens = images * tile_rows * tile_cols

    def project():
        flattened = modulate(hidden, shift_scale).reshape(tokens, D)
        queries = jnp.dot(flattened, weight_q, preferred_element_type=jnp.float32).astype(
            jnp.bfloat16
        )
        key_values = jnp.dot(flattened, weight_kv, preferred_element_type=jnp.float32).astype(
            jnp.bfloat16
        )
        return (queries, key_values)

    def nothing():
        return (jnp.zeros((tokens, HW), jnp.bfloat16), jnp.zeros((tokens, 2 * HW), jnp.bfloat16))

    queries, key_values = lax.cond(active, project, nothing)
    extended = edge_keys(key_values.reshape(images, tile_rows, tile_cols, 2 * HW))
    row_anchor = lax.axis_index("trow") * tile_rows
    col_anchor = lax.axis_index("tcol") * tile_cols
    total_rows = tile_rows * lax.axis_size("trow")
    total_cols = tile_cols * lax.axis_size("tcol")

    def finish():
        attended = attend_tile(
            queries.reshape(images, tile_rows, tile_cols, HW),
            extended,
            row_anchor,
            col_anchor,
            total_rows,
            total_cols,
        )
        projected = jnp.dot(
            attended.reshape(tokens, HW), weight_o, preferred_element_type=jnp.float32
        )
        return (hidden + shift_scale[2] * projected.reshape(hidden.shape)).astype(jnp.bfloat16)

    def vacant():
        return jnp.zeros(hidden.shape, jnp.bfloat16)

    return lax.cond(active, finish, vacant)


def zero_project(control_out, weight_z):
    flattened = control_out.reshape(-1, D)
    return (
        jnp.dot(flattened, weight_z, preferred_element_type=jnp.float32)
        .astype(jnp.bfloat16)
        .reshape(control_out.shape)
    )


def on_device(latent, modulation, w_query, w_keyval, w_out, w_zero):
    sources = (w_query, w_keyval, w_out)
    weight_q, weight_kv, weight_o, weight_z = (
        lax.all_gather(sources[0], "tcol", axis=2, tiled=True),
        lax.all_gather(sources[1], "tcol", axis=2, tiled=True),
        lax.all_gather(sources[2], "tcol", axis=1, tiled=True),
        lax.all_gather(w_zero, "tcol", axis=1, tiled=True),
    )
    branch_index = lax.axis_index("branch")
    is_control = branch_index == 1
    own_copy = latent[0]
    shift_scale = lax.dynamic_index_in_dim(modulation, branch_index, 0, keepdims=False)
    received = shifted(own_copy, "branch", 1)
    control_in = own_copy.astype(jnp.float32) + received.astype(jnp.float32)
    control_out = run_block(
        is_control, control_in, shift_scale, weight_q[0], weight_kv[0], weight_o[0]
    )

    def with_projection():
        return zero_project(control_out, weight_z)

    def without_projection():
        return jnp.zeros(control_out.shape, jnp.bfloat16)

    residual = lax.cond(is_control, with_projection, without_projection)
    returned = shifted(residual, "branch", -1)
    base_in = own_copy.astype(jnp.float32) + returned.astype(jnp.float32)
    base_out = run_block(
        jnp.logical_not(is_control), base_in, shift_scale, weight_q[0], weight_kv[0], weight_o[0]
    )
    return jnp.where(is_control, control_out, base_out)[None]


def solution(mesh):
    placed = (
        P("branch", None, "trow", "tcol", None),
        P(),
        P("branch", None, "tcol"),
        P("branch", None, "tcol"),
        P("branch", "tcol", None),
        P(None, "tcol"),
    )
    return jax.shard_map(
        on_device,
        mesh=mesh,
        in_specs=placed,
        out_specs=P("branch", None, "trow", "tcol", None),
        check_vma=False,
    )
```

profile of v0, /device:TPU:1, one launch (start us, length us, event | category | flops | bytes accessed | tf_op | source)
XLA Modules:
  0.0 417.9 jit_solution(13802482478232100090)
XLA Ops:
  6.5 1.5 copy.65
  8.1 1.7 copy.66
  9.9 1.5 copy.73
  11.5 0.5 all-gather.12.cloned.1.call-update
  12.0 8.3 %collective-permute-start = (bf16[2,8,8,1152]{3,2,1,0:T(8,128)(2,1)}, bf16[2,8,8,1152]{3,2,1,0:T(8,128)(2,1)S(1)}, u32[]{:S(2)}, u32[]{:S(2)}) collective-permute-start(bf16[2,8,8,1152]{3,2,1,0:T(8,128)(2,1)} %bitcast.100), channel_id=1, source_target_pairs={{0,256},{1,257},{2,258},{3,259},{4,260},{5,261},{6,262},{7,263},{8... | collective-permute-start | bytes 884744 | tf_op jit(solution)/shard_map/ppermute | solution.py:30
  20.4 5.9 %collective-permute-done = bf16[2,8,8,1152]{3,2,1,0:T(8,128)(2,1)S(1)} collective-permute-done((bf16[2,8,8,1152]{3,2,1,0:T(8,128)(2,1)}, bf16[2,8,8,1152]{3,2,1,0:T(8,128)(2,1)S(1)}, u32[]{:S(2)}, u32[]{:S(2)}) %collective-permute-start) | collective-permute-done | bytes 294944 | tf_op jit(solution)/shard_map/ppermute | solution.py:30
  26.3 1.0 convert_add_fusion.1
  27.3 51.8 %all-gather.6.cloned.1.call-done = bf16[1,1152,576]{1,0,2:T(2,128)(2,1)} async-done(((bf16[1,1152,18]{1,0,2:T(2,128)(2,1)}), bf16[1,1152,576]{1,0,2:T(2,128)(2,1)}) %all-gather.6.cloned.1.call-update) | async-done | bytes 1327120 | tf_op jit(solution)/shard_map/all_gather | solution.py:169
  79.1 3.0 copy.120
  82.1 68.8 %all-gather.8.cloned.1.call-done = bf16[1,1152,1152]{1,0,2:T(2,128)(2,1)} async-done(((bf16[1,1152,36]{1,0,2:T(2,128)(2,1)}), bf16[1,1152,1152]{1,0,2:T(2,128)(2,1)}) %all-gather.8.cloned.1.call-update) | async-done | bytes 2654224 | tf_op jit(solution)/shard_map/all_gather | solution.py:170
  150.9 10.9 %copy.67 = bf16[1,1152,1152]{2,1,0:T(8,128)(2,1)S(1)} copy(bf16[1,1152,1152]{1,0,2:T(2,128)(2,1)} %all-gather.8.cloned.1.call-done) | data formatting | bytes 5308416 | tf_op jit(solution)/shard_map/all_gather | solution.py:170
  161.8 0.8 conditional.5
  161.8 0.7 broadcast.427
  162.6 1.1 fusion.47
  163.7 1.3 collective-permute-start.2
  165.0 4.0 collective-permute-start.1
  169.0 3.3 collective-permute-done.2
  172.4 0.9 collective-permute-done.1
  173.2 0.7 copy-done.3
  173.9 1.1 pad_maximum_fusion.2
  175.2 1.2 copy.70
  176.4 3.3 collective-permute-start.4
  179.8 1.2 copy.69
  181.0 2.5 collective-permute-start.3
  183.5 38.2 %all-gather.10.cloned.1.call-done = bf16[1,576,1152]{2,0,1:T(2,128)(2,1)} async-done(((bf16[1,18,1152]{2,0,1:T(2,128)(2,1)}), bf16[1,576,1152]{2,0,1:T(2,128)(2,1)}) %all-gather.10.cloned.1.call-update) | async-done | bytes 1327120 | tf_op jit(solution)/shard_map/all_gather | solution.py:171
  221.7 3.0 copy.119
  224.7 63.1 %all-gather.12.cloned.1.call-done = bf16[32,36,1152]{2,1,0:T(8,128)(2,1)} async-done(((bf16[1,36,1152]{2,1,0:T(8,128)(2,1)}), bf16[32,36,1152]{2,1,0:T(8,128)(2,1)}) %all-gather.12.cloned.1.call-update) | async-done | bytes 2654224 | tf_op jit(solution)/shard_map/all_gather | solution.py:172
  287.8 5.2 %reshape.395 = bf16[1152,1152]{1,0:T(8,128)(2,1)} reshape(bf16[32,36,1152]{2,1,0:T(8,128)(2,1)} %all-gather.12.cloned.1.call-done) | data formatting | bytes 5308416
  293.0 1.2 copy.72
  294.2 1.1 copy.71
  295.3 3.0 pad_maximum_fusion
  298.3 0.7 conditional.6
  298.3 0.7 broadcast.431
  299.0 0.2 conditional.7
  299.2 1.3 collective-permute-start.5
  300.6 41.7 %collective-permute-done.5 = bf16[2,8,8,1152]{3,2,1,0:T(8,128)(2,1)} collective-permute-done((bf16[2,8,8,1152]{3,2,1,0:T(8,128)(2,1)S(1)}, bf16[2,8,8,1152]{3,2,1,0:T(8,128)(2,1)}, u32[]{:S(2)}, u32[]{:S(2)}) %collective-permute-start.5) | collective-permute-done | bytes 294944 | tf_op jit(solution)/shard_map/ppermute | solution.py:30
  342.3 1.1 convert_add_fusion
  343.4 3.7 conditional.8
  343.6 0.2 multiply_reduce_fusion.1
  344.0 1.8 convolution_convert_fusion.5
  345.8 1.3 convolution_convert_fusion.4
  347.1 1.1 fusion.46
  348.2 1.3 collective-permute-start.7
  349.5 4.0 collective-permute-start.6
  353.5 2.6 collective-permute-done.7
  356.2 0.9 collective-permute-done.6
  357.0 1.1 pad_maximum_fusion.3
  358.3 0.4 copy.79
  358.7 4.0 collective-permute-start.9
  362.7 0.4 copy.78
  363.2 8.5 %collective-permute-start.8 = (bf16[2,20,6,1152]{3,0,2,1:T(2,128)(2,1)S(1)}, bf16[2,20,6,1152]{3,0,2,1:T(2,128)(2,1)S(1)}, u32[]{:S(2)}, u32[]{:S(2)}) collective-permute-start(bf16[2,20,6,1152]{3,0,2,1:T(2,128)(2,1)S(1)} %copy.78), channel_id=1, source_target_pairs={{0,1},{1,2},{2,3},{3,4},{4,5},{5,6},{6,7},{7,8},{8,9},{9,10},{10,1... | collective-permute-start | bytes 1658888 | tf_op jit(solution)/shard_map/ppermute | solution.py:19
  371.7 9.8 %collective-permute-done.9 = bf16[2,20,6,1152]{3,0,2,1:T(2,128)(2,1)S(1)} collective-permute-done((bf16[2,20,6,1152]{3,0,2,1:T(2,128)(2,1)S(1)}, bf16[2,20,6,1152]{3,0,2,1:T(2,128)(2,1)S(1)}, u32[]{:S(2)}, u32[]{:S(2)}) %collective-permute-start.9) | collective-permute-done | bytes 552992 | tf_op jit(solution)/shard_map/ppermute | solution.py:22
  381.7 3.1 pad_maximum_fusion.1
  384.8 24.9 %conditional.9 = (bf16[2,8,8,1152]{3,2,1,0:T(8,128)(2,1)}) conditional(s32[]{:T(128)} %convert_element_type.76, () %tuple.47, (f32[3,1152]{1,0:T(4,128)S(1)}, bf16[2,20,20,1152]{3,2,1,0:T(8,128)(2,1)}, s32[]{:T(128)}, s32[]{:T(128)}, bf16[128,576]{0,1:T(8,128)(2,1)S(1)}, /*index=5*/bf16[576,1152]{1,0:T(8,128)(2,1)S(1)}, ...), branch_computations={%region_14.15_spmd, %region_15.18_spmd} | conditional | flops 324553312 | bytes 28789580 | solution.py:154
  384.8 3.1 copy.82
  387.9 5.6 %pad_slice_fusion.2 = (bf16[2,512,576]{2,0,1:T(2,128)(2,1)S(1)}, bf16[2,512,576]{2,0,1:T(2,128)(2,1)}) fusion(bf16[2,400,1152]{2,0,1:T(2,128)(2,1)S(1)} %bitcast.91), kind=kLoop, calls=%fused_computation.55 | loop fusion | bytes 4202496 | tf_op jit(solution)/shard_map/cond/branch_1_fun/while/body/eval_jaxpr/slice | solution.py:87
  393.5 4.2 %copy.61 = bf16[2,512,576]{1,2,0:T(8,128)(2,1)} copy(bf16[2,512,576]{2,0,1:T(2,128)(2,1)} %get-tuple-element.221) | data formatting | bytes 2359296 | tf_op jit(solution)/shard_map/cond/branch_1_fun/while/body/eval_jaxpr/slice | solution.py:88
  398.1 0.3 and.96
  398.4 3.1 copy.62
  401.6 0.9 reshape.399
  402.4 3.6 fusion.41
  406.0 2.2 fusion.24
  408.6 1.1 fusion.21
  409.7 1.7 select_bitcast_fusion
  (49 shorter events, 1.9 us)
Async XLA Ops:
  6.5 13.8 %copy-start = (f32[2,3,1152]{2,0,1:T(2,128)S(1)}, f32[2,3,1152]{2,0,1:T(2,128)}, u32[]{:S(2)}) copy-start(f32[2,3,1152]{2,0,1:T(2,128)} %param.17) | copy-start | bytes 82948
  6.5 72.6 %all-gather.6.cloned.1.call-start = ((), (), s32[]{:S(2)}) async-start(), calls=%async_computation | async-start | bytes 2737152 | tf_op jit(solution)/shard_map/all_gather | solution.py:169
  8.1 142.8 %all-gather.8.cloned.1.call-start = ((), (), s32[]{:S(2)}) async-start(), calls=%async_computation.1 | async-start | bytes 5474304 | tf_op jit(solution)/shard_map/all_gather | solution.py:170
  9.8 211.8 %all-gather.10.cloned.1.call-start = ((), (), s32[]{:S(2)}) async-start(), calls=%async_computation.2 | async-start | bytes 2737152 | tf_op jit(solution)/shard_map/all_gather | solution.py:171
  11.4 276.4 %all-gather.12.cloned.1.call-start = ((), (), s32[]{:S(2)}) async-start(), calls=%async_computation.3 | async-start | bytes 3041280 | tf_op jit(solution)/shard_map/all_gather | solution.py:172
  12.0 14.3 %collective-permute-start = (bf16[2,8,8,1152]{3,2,1,0:T(8,128)(2,1)}, bf16[2,8,8,1152]{3,2,1,0:T(8,128)(2,1)S(1)}, u32[]{:S(2)}, u32[]{:S(2)}) collective-permute-start(bf16[2,8,8,1152]{3,2,1,0:T(8,128)(2,1)} %bitcast.100), channel_id=1, source_target_pairs={{0,256},{1,257},{2,258},{3,259},{4,260},{5,261},{6,262},{7,263},{8... | collective-permute-start | bytes 884744 | tf_op jit(solution)/shard_map/ppermute | solution.py:30
  162.6 1.1 copy-start.5
  163.7 8.6 %collective-permute-start.2 = (bf16[2,6,8,1152]{3,2,1,0:T(8,128)(2,1)S(1)}, bf16[2,6,8,1152]{3,2,1,0:T(8,128)(2,1)S(1)}, u32[]{:S(2)}, u32[]{:S(2)}) collective-permute-start(bf16[2,6,8,1152]{3,2,1,0:T(8,128)(2,1)S(1)} %get-tuple-element.235), channel_id=1, source_target_pairs={{32,0},{64,32},{96,64},{128,96},{160,128},{192,160},{224,192},{33,... | collective-permute-start | bytes 663560 | tf_op jit(solution)/shard_map/ppermute | solution.py:22
  165.0 8.2 %collective-permute-start.1 = (bf16[2,6,8,1152]{3,2,1,0:T(8,128)(2,1)S(1)}, bf16[2,6,8,1152]{3,2,1,0:T(8,128)(2,1)S(1)}, u32[]{:S(2)}, u32[]{:S(2)}) collective-permute-start(bf16[2,6,8,1152]{3,2,1,0:T(8,128)(2,1)S(1)} %get-tuple-element.234), channel_id=1, source_target_pairs={{0,32},{32,64},{64,96},{96,128},{128,160},{160,192},{192,224},{1,3... | collective-permute-start | bytes 663560 | tf_op jit(solution)/shard_map/ppermute | solution.py:19
  173.2 0.7 copy-start.3
  176.4 116.6 %collective-permute-start.4 = (bf16[2,20,6,1152]{3,0,2,1:T(2,128)(2,1)}, bf16[2,20,6,1152]{3,0,2,1:T(2,128)(2,1)}, u32[]{:S(2)}, u32[]{:S(2)}) collective-permute-start(bf16[2,20,6,1152]{3,0,2,1:T(2,128)(2,1)} %copy.70), channel_id=1, source_target_pairs={{1,0},{2,1},{3,2},{4,3},{5,4},{6,5},{7,6},{8,7},{9,8},{10,9},{11,1... | collective-permute-start | bytes 1658888 | tf_op jit(solution)/shard_map/ppermute | solution.py:22
  181.0 113.2 %collective-permute-start.3 = (bf16[2,20,6,1152]{3,0,2,1:T(2,128)(2,1)}, bf16[2,20,6,1152]{3,0,2,1:T(2,128)(2,1)}, u32[]{:S(2)}, u32[]{:S(2)}) collective-permute-start(bf16[2,20,6,1152]{3,0,2,1:T(2,128)(2,1)} %copy.69), channel_id=1, source_target_pairs={{0,1},{1,2},{2,3},{3,4},{4,5},{5,6},{6,7},{7,8},{8,9},{9,10},{10,1... | collective-permute-start | bytes 1658888 | tf_op jit(solution)/shard_map/ppermute | solution.py:19
  293.0 2.3 copy-start.4
  299.2 43.0 %collective-permute-start.5 = (bf16[2,8,8,1152]{3,2,1,0:T(8,128)(2,1)S(1)}, bf16[2,8,8,1152]{3,2,1,0:T(8,128)(2,1)}, u32[]{:S(2)}, u32[]{:S(2)}) collective-permute-start(bf16[2,8,8,1152]{3,2,1,0:T(8,128)(2,1)S(1)} %get-tuple-element.245), channel_id=1, source_target_pairs={{256,0},{257,1},{258,2},{259,3},{260,4},{261,5},{262,6},{263,7},{2... | collective-permute-start | bytes 884744 | tf_op jit(solution)/shard_map/ppermute | solution.py:30
  348.2 7.9 %collective-permute-start.7 = (bf16[2,6,8,1152]{3,2,1,0:T(8,128)(2,1)S(1)}, bf16[2,6,8,1152]{3,2,1,0:T(8,128)(2,1)S(1)}, u32[]{:S(2)}, u32[]{:S(2)}) collective-permute-start(bf16[2,6,8,1152]{3,2,1,0:T(8,128)(2,1)S(1)} %get-tuple-element.233), channel_id=1, source_target_pairs={{32,0},{64,32},{96,64},{128,96},{160,128},{192,160},{224,192},{33,... | collective-permute-start | bytes 663560 | tf_op jit(solution)/shard_map/ppermute | solution.py:22
  349.5 7.5 %collective-permute-start.6 = (bf16[2,6,8,1152]{3,2,1,0:T(8,128)(2,1)S(1)}, bf16[2,6,8,1152]{3,2,1,0:T(8,128)(2,1)S(1)}, u32[]{:S(2)}, u32[]{:S(2)}) collective-permute-start(bf16[2,6,8,1152]{3,2,1,0:T(8,128)(2,1)S(1)} %get-tuple-element.232), channel_id=1, source_target_pairs={{0,32},{32,64},{64,96},{96,128},{128,160},{160,192},{192,224},{1,3... | collective-permute-start | bytes 663560 | tf_op jit(solution)/shard_map/ppermute | solution.py:19
  358.7 22.8 %collective-permute-start.9 = (bf16[2,20,6,1152]{3,0,2,1:T(2,128)(2,1)S(1)}, bf16[2,20,6,1152]{3,0,2,1:T(2,128)(2,1)S(1)}, u32[]{:S(2)}, u32[]{:S(2)}) collective-permute-start(bf16[2,20,6,1152]{3,0,2,1:T(2,128)(2,1)S(1)} %copy.79), channel_id=1, source_target_pairs={{1,0},{2,1},{3,2},{4,3},{5,4},{6,5},{7,6},{8,7},{9,8},{10,9},{11,1... | collective-permute-start | bytes 1658888 | tf_op jit(solution)/shard_map/ppermute | solution.py:22
  363.2 18.4 %collective-permute-start.8 = (bf16[2,20,6,1152]{3,0,2,1:T(2,128)(2,1)S(1)}, bf16[2,20,6,1152]{3,0,2,1:T(2,128)(2,1)S(1)}, u32[]{:S(2)}, u32[]{:S(2)}) collective-permute-start(bf16[2,20,6,1152]{3,0,2,1:T(2,128)(2,1)S(1)} %copy.78), channel_id=1, source_target_pairs={{0,1},{1,2},{2,3},{3,4},{4,5},{5,6},{6,7},{7,8},{8,9},{9,10},{10,1... | collective-permute-start | bytes 1658888 | tf_op jit(solution)/shard_map/ppermute | solution.py:19
  381.7 3.1 copy-start.1
  384.8 8.7 %copy-start.7 = (bf16[128,576]{0,1:T(8,128)(2,1)}, bf16[128,576]{0,1:T(8,128)(2,1)S(1)}, u32[]{:S(2)}) copy-start(bf16[128,576]{0,1:T(8,128)(2,1)S(1)} %get-tuple-element.205) | copy-start | bytes 442372 | tf_op jit(solution)/shard_map/cond
  398.4 3.2 copy-start.8
  402.4 3.6 copy-start.2
Sparse Core Ops, SparseCore 0:
  9.5 69.5 all-gather.5
  81.3 69.5 all-gather.7
  153.1 68.5 all-gather.9
  223.7 64.0 all-gather.11
where the time goes:
time: 419 us; the launch traced here: 418 us
  waiting for transfers between devices  288 us (69%)
  local copies, waits for them, and re-layouts  55 us (13%)
  starting transfers between devices  38.7 us (9%)
  between operations  13.4 us (3%)
  other arithmetic  12.9 us (3%)
  matrix products  9.98 us (2%)
    all_gather x1, waiting for transfers between devices, on_device(): lax.all_gather(sources[1], 'tcol', axis=2, tiled=True)  68.8 us
    all_gather x1, waiting for transfers between devices, on_device(): lax.all_gather(w_zero, 'tcol', axis=1, tiled=True)  63.1 us
    all_gather x1, waiting for transfers between devices, on_device(): lax.all_gather(sources[0], 'tcol', axis=2, tiled=True)  51.8 us
    ppermute x2, waiting for transfers between devices, shifted(): return lax.ppermute(block, axis, route)  47.6 us
    all_gather x1, waiting for transfers between devices, on_device(): lax.all_gather(sources[2], 'tcol', axis=1, tiled=True)  38.2 us
    ppermute x4, starting transfers between devices, padded(): lax.ppermute(lax.slice_in_dim(block, block.shape[dim] - width, None, axis...  19.1 us
    unnamed x17, local copies, waits for them, and re-layouts  16.6 us
    ppermute x4, waiting for transfers between devices, padded(): lax.ppermute(lax.slice_in_dim(block, 0, width, axis=dim), axis, backward)  15.8 us
  transfers between devices with their start and end apart: 14, of which 11 were waited for; matrix products, arithmetic and copies ran while one was open for 8% of the time, Pallas kernels for 0%

commit v1 on v0

--- a/solution.py
+++ b/solution.py
@@ -9,6 +9,12 @@
 HEADS = 8
 WIN = 13
 HW = 576
+
+
+def _produce_zone(unit):
+    return jnp.concatenate(
+        lax.all_to_all(jnp.stack(lax.axis_size("tcol") * [unit], axis=0), "tcol", 0, 0), axis=1
+    )
 
 
 def padded(block, sides, width):
@@ -168,7 +174,7 @@
     weight_q, weight_kv, weight_o, weight_z = (
         lax.all_gather(sources[0], "tcol", axis=2, tiled=True),
         lax.all_gather(sources[1], "tcol", axis=2, tiled=True),
-        lax.all_gather(sources[2], "tcol", axis=1, tiled=True),
+        _produce_zone(sources[2]),
         lax.all_gather(w_zero, "tcol", axis=1, tiled=True),
     )
     branch_index = lax.axis_index("branch")

time: 419 us -> 371 us (0.89)
  waiting for transfers between devices: 288 us -> 232 us
  starting transfers between devices: 38.7 us -> 45.4 us
    all_gather x1 -> x0, waiting for transfers between devices: 38.2 us -> none  [on_device(): lax.all_gather(sources[2], 'tcol', axis=1, tiled=True)]
    all_gather x1, waiting for transfers between devices: 63.1 us -> 35.1 us  [on_device(): lax.all_gather(w_zero, 'tcol', axis=1, tiled=True)]
    all_gather x1, waiting for transfers between devices: 51.8 us -> 66.9 us  [on_device(): lax.all_gather(sources[0], 'tcol', axis=2, tiled=True)]
    ppermute x2, waiting for transfers between devices: 47.6 us -> 41.7 us  [shifted(): return lax.ppermute(block, axis, route)]
    all_to_all x0 -> x1, starting transfers between devices: none -> 5.93 us  [_produce_zone(): lax.all_to_all(jnp.stack(lax.axis_size('tcol') * [unit], axis=0), 'tcol',...]
    another operation x5 -> x7, local copies, waits for them, and re-layouts: 4.62 us -> 10.3 us
    unnamed x17, local copies, waits for them, and re-layouts: 16.6 us -> 12.1 us
  transfers between devices with their start and end apart: 14 -> 14, of which waited for: 11 -> 9; matrix products, arithmetic and copies ran while one was open for 8% -> 9% of each run, Pallas kernels for 0% -> 0%
where the time goes in v1:
time: 371 us; the launch traced here: 369 us
  waiting for transfers between devices  232 us (63%)
  local copies, waits for them, and re-layouts  56.2 us (15%)
  starting transfers between devices  45.4 us (12%)
  between operations  13.4 us (4%)
  other arithmetic  11.9 us (3%)
  matrix products  9.95 us (3%)
    all_gather x1, waiting for transfers between devices, on_device(): lax.all_gather(sources[1], 'tcol', axis=2, tiled=True)  69.6 us
    all_gather x1, waiting for transfers between devices, on_device(): lax.all_gather(sources[0], 'tcol', axis=2, tiled=True)  66.9 us
    ppermute x2, waiting for transfers between devices, shifted(): return lax.ppermute(block, axis, route)  41.7 us
    all_gather x1, waiting for transfers between devices, on_device(): lax.all_gather(w_zero, 'tcol', axis=1, tiled=True)  35.1 us
    ppermute x4, starting transfers between devices, padded(): lax.ppermute(lax.slice_in_dim(block, block.shape[dim] - width, None, axis...  19.9 us
    ppermute x4, waiting for transfers between devices, padded(): lax.ppermute(lax.slice_in_dim(block, 0, width, axis=dim), axis, backward)  16.3 us
    unnamed x17, local copies, waits for them, and re-layouts  12.1 us
    all_gather x1, local copies, waits for them, and re-layouts, on_device(): lax.all_gather(sources[1], 'tcol', axis=2, tiled=True)  10.9 us
  transfers between devices with their start and end apart: 14, of which 9 were waited for; matrix products, arithmetic and copies ran while one was open for 9% of the time, Pallas kernels for 0%

profile of v1, /device:TPU:1, one launch (start us, length us, event | category | flops | bytes accessed | tf_op | source)
XLA Modules:
  0.0 369.1 jit_solution(7188406583961342149)
XLA Ops:
  6.5 1.5 copy.64
  8.1 1.7 copy.65
  9.9 0.7 all-gather.9.cloned.1.call-update
  10.6 8.3 %collective-permute-start = (bf16[2,8,8,1152]{3,2,1,0:T(8,128)(2,1)}, bf16[2,8,8,1152]{3,2,1,0:T(8,128)(2,1)S(1)}, u32[]{:S(2)}, u32[]{:S(2)}) collective-permute-start(bf16[2,8,8,1152]{3,2,1,0:T(8,128)(2,1)} %bitcast.96), channel_id=1, source_target_pairs={{0,256},{1,257},{2,258},{3,259},{4,260},{5,261},{6,262},{7,263},{8... | collective-permute-start | bytes 884744 | tf_op jit(solution)/shard_map/ppermute | solution.py:36
  18.9 2.2 stack.2
  21.1 5.9 %all-to-all-start = ((bf16[32,1,18,1152]{3,2,1,0:T(8,128)(2,1)}), bf16[32,1,18,1152]{3,2,1,0:T(8,128)(2,1)}, u32[]{:S(2)}, u32[]{:S(2)}) async-start(bf16[32,1,18,1152]{3,2,1,0:T(8,128)(2,1)} %stack.2), calls=%async_computation | async-start | bytes 3538944 | tf_op jit(solution)/shard_map/all_to_all | solution.py:16
  27.2 66.9 %all-gather.5.cloned.1.call-done = bf16[1,1152,576]{1,0,2:T(2,128)(2,1)} async-done(((bf16[1,1152,18]{1,0,2:T(2,128)(2,1)}), bf16[1,1152,576]{1,0,2:T(2,128)(2,1)}) %all-gather.5.cloned.1.call-update) | async-done | bytes 1327120 | tf_op jit(solution)/shard_map/all_gather | solution.py:175
  94.0 3.0 copy.115
  97.0 69.6 %all-gather.7.cloned.1.call-done = bf16[1,1152,1152]{1,0,2:T(2,128)(2,1)} async-done(((bf16[1,1152,36]{1,0,2:T(2,128)(2,1)}), bf16[1,1152,1152]{1,0,2:T(2,128)(2,1)}) %all-gather.7.cloned.1.call-update) | async-done | bytes 2654224 | tf_op jit(solution)/shard_map/all_gather | solution.py:176
  166.6 10.9 %copy.66 = bf16[1,1152,1152]{2,1,0:T(8,128)(2,1)S(1)} copy(bf16[1,1152,1152]{1,0,2:T(2,128)(2,1)} %all-gather.7.cloned.1.call-done) | data formatting | bytes 5308416 | tf_op jit(solution)/shard_map/all_gather | solution.py:176
  177.5 0.8 conditional.5
  177.6 0.7 broadcast.430
  178.3 1.1 fusion.47
  179.4 1.3 collective-permute-start.2
  180.7 4.0 %collective-permute-start.1 = (bf16[2,6,8,1152]{3,2,1,0:T(8,128)(2,1)S(1)}, bf16[2,6,8,1152]{3,2,1,0:T(8,128)(2,1)S(1)}, u32[]{:S(2)}, u32[]{:S(2)}) collective-permute-start(bf16[2,6,8,1152]{3,2,1,0:T(8,128)(2,1)S(1)} %get-tuple-element.234), channel_id=1, source_target_pairs={{0,32},{32,64},{64,96},{96,128},{128,160},{160,192},{192,224},{1,3... | collective-permute-start | bytes 663560 | tf_op jit(solution)/shard_map/ppermute | solution.py:25
  184.8 3.3 collective-permute-done.2
  188.1 0.9 collective-permute-done.1
  189.0 0.7 copy-done.4
  189.7 1.1 pad_maximum_fusion.2
  190.7 0.2 fusion.45
  190.9 1.2 copy.69
  192.2 3.3 collective-permute-start.4
  195.5 1.2 copy.68
  196.7 2.4 collective-permute-start.3
  199.2 3.5 squeeze_reshape.4
  202.6 35.1 %all-gather.9.cloned.1.call-done = bf16[32,36,1152]{2,1,0:T(8,128)(2,1)} async-done(((bf16[1,36,1152]{2,1,0:T(8,128)(2,1)}), bf16[32,36,1152]{2,1,0:T(8,128)(2,1)}) %all-gather.9.cloned.1.call-update) | async-done | bytes 2654224 | tf_op jit(solution)/shard_map/all_gather | solution.py:178
  237.8 5.2 %reshape.398 = bf16[1152,1152]{1,0:T(8,128)(2,1)} reshape(bf16[32,36,1152]{2,1,0:T(8,128)(2,1)} %all-gather.9.cloned.1.call-done) | data formatting | bytes 5308416
  242.9 1.2 copy.71
  244.1 1.1 copy.70
  245.3 3.0 pad_maximum_fusion
  248.2 0.7 conditional.6
  248.2 0.7 broadcast.434
  249.0 1.3 collective-permute-start.5
  250.3 41.7 %collective-permute-done.5 = bf16[2,8,8,1152]{3,2,1,0:T(8,128)(2,1)} collective-permute-done((bf16[2,8,8,1152]{3,2,1,0:T(8,128)(2,1)S(1)}, bf16[2,8,8,1152]{3,2,1,0:T(8,128)(2,1)}, u32[]{:S(2)}, u32[]{:S(2)}) %collective-permute-start.5) | collective-permute-done | bytes 294944 | tf_op jit(solution)/shard_map/ppermute | solution.py:36
  292.0 1.1 convert_add_fusion
  293.1 3.7 %conditional.8 = (bf16[128,576]{0,1:T(8,128)(2,1)S(1)}, bf16[128,1152]{1,0:T(8,128)(2,1)}) conditional(s32[]{:T(128)} %convert_element_type.76, () %tuple.48, (f32[2,8,8,1152]{3,2,1,0:T(8,128)S(1)}, f32[3,1152]{1,0:T(4,128)S(1)}, bf16[1152,576]{0,1:T(8,128)(2,1)}, bf16[1152,1152]{1,0:T(8,128)(2,1)S(1)}) %tuple.107), branch_computations={%region_10.11_spmd, %region_11.14_spmd} | conditional | flops 511157504 | bytes 7110164 | solution.py:136
  293.3 0.2 multiply_reduce_fusion.1
  293.7 1.8 convolution_convert_fusion.5
  295.5 1.3 convolution_convert_fusion.4
  296.8 1.1 fusion.46
  297.9 1.3 collective-permute-start.7
  299.2 4.0 %collective-permute-start.6 = (bf16[2,6,8,1152]{3,2,1,0:T(8,128)(2,1)S(1)}, bf16[2,6,8,1152]{3,2,1,0:T(8,128)(2,1)S(1)}, u32[]{:S(2)}, u32[]{:S(2)}) collective-permute-start(bf16[2,6,8,1152]{3,2,1,0:T(8,128)(2,1)S(1)} %get-tuple-element.232), channel_id=1, source_target_pairs={{0,32},{32,64},{64,96},{96,128},{128,160},{160,192},{192,224},{1,3... | collective-permute-start | bytes 663560 | tf_op jit(solution)/shard_map/ppermute | solution.py:25
  303.2 2.6 collective-permute-done.7
  305.9 0.9 collective-permute-done.6
  306.7 1.1 pad_maximum_fusion.3
  307.8 0.2 fusion.44
  308.0 0.4 copy.77
  308.4 4.0 %collective-permute-start.9 = (bf16[2,20,6,1152]{3,0,2,1:T(2,128)(2,1)S(1)}, bf16[2,20,6,1152]{3,0,2,1:T(2,128)(2,1)S(1)}, u32[]{:S(2)}, u32[]{:S(2)}) collective-permute-start(bf16[2,20,6,1152]{3,0,2,1:T(2,128)(2,1)S(1)} %copy.77), channel_id=1, source_target_pairs={{1,0},{2,1},{3,2},{4,3},{5,4},{6,5},{7,6},{8,7},{9,8},{10,9},{11,1... | collective-permute-start | bytes 1658888 | tf_op jit(solution)/shard_map/ppermute | solution.py:28
  312.5 0.4 copy.76
  312.9 9.5 %collective-permute-start.8 = (bf16[2,20,6,1152]{3,0,2,1:T(2,128)(2,1)S(1)}, bf16[2,20,6,1152]{3,0,2,1:T(2,128)(2,1)S(1)}, u32[]{:S(2)}, u32[]{:S(2)}) collective-permute-start(bf16[2,20,6,1152]{3,0,2,1:T(2,128)(2,1)S(1)} %copy.76), channel_id=1, source_target_pairs={{0,1},{1,2},{2,3},{3,4},{4,5},{5,6},{6,7},{7,8},{8,9},{9,10},{10,1... | collective-permute-start | bytes 1658888 | tf_op jit(solution)/shard_map/ppermute | solution.py:25
  322.4 10.3 %collective-permute-done.9 = bf16[2,20,6,1152]{3,0,2,1:T(2,128)(2,1)S(1)} collective-permute-done((bf16[2,20,6,1152]{3,0,2,1:T(2,128)(2,1)S(1)}, bf16[2,20,6,1152]{3,0,2,1:T(2,128)(2,1)S(1)}, u32[]{:S(2)}, u32[]{:S(2)}) %collective-permute-start.9) | collective-permute-done | bytes 552992 | tf_op jit(solution)/shard_map/ppermute | solution.py:28
  332.9 3.1 pad_maximum_fusion.1
  336.0 24.9 %conditional.9 = (bf16[2,8,8,1152]{3,2,1,0:T(8,128)(2,1)}) conditional(s32[]{:T(128)} %convert_element_type.76, () %tuple.47, (f32[3,1152]{1,0:T(4,128)S(1)}, bf16[2,20,20,1152]{3,2,1,0:T(8,128)(2,1)}, s32[]{:T(128)}, s32[]{:T(128)}, bf16[128,576]{0,1:T(8,128)(2,1)S(1)}, /*index=5*/bf16[576,1152]{1,0:T(8,128)(2,1)S(1)}, ...), branch_computations={%region_14.15_spmd, %region_15.18_spmd} | conditional | flops 324553312 | bytes 28789580 | solution.py:160
  336.0 3.1 copy.80
  339.1 5.6 %pad_slice_fusion.2 = (bf16[2,512,576]{2,0,1:T(2,128)(2,1)S(1)}, bf16[2,512,576]{2,0,1:T(2,128)(2,1)}) fusion(bf16[2,400,1152]{2,0,1:T(2,128)(2,1)S(1)} %bitcast.87), kind=kLoop, calls=%fused_computation.55 | loop fusion | bytes 4202496 | tf_op jit(solution)/shard_map/cond/branch_1_fun/while/body/eval_jaxpr/slice | solution.py:93
  344.7 4.2 %copy.60 = bf16[2,512,576]{1,2,0:T(8,128)(2,1)} copy(bf16[2,512,576]{2,0,1:T(2,128)(2,1)} %get-tuple-element.221) | data formatting | bytes 2359296 | tf_op jit(solution)/shard_map/cond/branch_1_fun/while/body/eval_jaxpr/slice | solution.py:94
  349.3 0.3 and.96
  349.6 3.1 copy.61
  352.7 0.9 reshape.402
  353.6 3.6 fusion.41
  357.1 2.1 fusion.24
  359.5 0.2 dot_general.39
  359.7 1.1 fusion.21
  360.8 1.7 select_bitcast_fusion
  (50 shorter events, 1.4 us)
Async XLA Ops:
  6.5 20.5 %copy-start = (f32[2,3,1152]{2,0,1:T(2,128)S(1)}, f32[2,3,1152]{2,0,1:T(2,128)}, u32[]{:S(2)}) copy-start(f32[2,3,1152]{2,0,1:T(2,128)} %param.17) | copy-start | bytes 82948
  6.5 87.5 %all-gather.5.cloned.1.call-start = ((), (), s32[]{:S(2)}) async-start(), calls=%async_computation.1 | async-start | bytes 2737152 | tf_op jit(solution)/shard_map/all_gather | solution.py:175
  8.1 158.5 %all-gather.7.cloned.1.call-start = ((), (), s32[]{:S(2)}) async-start(), calls=%async_computation.2 | async-start | bytes 5474304 | tf_op jit(solution)/shard_map/all_gather | solution.py:176
  9.8 227.9 %all-gather.9.cloned.1.call-start = ((), (), s32[]{:S(2)}) async-start(), calls=%async_computation.3 | async-start | bytes 3041280 | tf_op jit(solution)/shard_map/all_gather | solution.py:178
  10.6 16.5 %collective-permute-start = (bf16[2,8,8,1152]{3,2,1,0:T(8,128)(2,1)}, bf16[2,8,8,1152]{3,2,1,0:T(8,128)(2,1)S(1)}, u32[]{:S(2)}, u32[]{:S(2)}) collective-permute-start(bf16[2,8,8,1152]{3,2,1,0:T(8,128)(2,1)} %bitcast.96), channel_id=1, source_target_pairs={{0,256},{1,257},{2,258},{3,259},{4,260},{5,261},{6,262},{7,263},{8... | collective-permute-start | bytes 884744 | tf_op jit(solution)/shard_map/ppermute | solution.py:36
  21.1 6.0 %copy-start.3 = (bf16[1,2,8,8,1152]{4,3,2,1,0:T(8,128)(2,1)S(1)}, bf16[1,2,8,8,1152]{4,3,2,1,0:T(8,128)(2,1)}, u32[]{:S(2)}) copy-start(bf16[1,2,8,8,1152]{4,3,2,1,0:T(8,128)(2,1)} %param.16) | copy-start | bytes 884740
  21.1 178.1 %all-to-all-start = ((bf16[32,1,18,1152]{3,2,1,0:T(8,128)(2,1)}), bf16[32,1,18,1152]{3,2,1,0:T(8,128)(2,1)}, u32[]{:S(2)}, u32[]{:S(2)}) async-start(bf16[32,1,18,1152]{3,2,1,0:T(8,128)(2,1)} %stack.2), calls=%async_computation | async-start | bytes 3538944 | tf_op jit(solution)/shard_map/all_to_all | solution.py:16
  178.3 1.1 copy-start.6
  179.4 8.6 %collective-permute-start.2 = (bf16[2,6,8,1152]{3,2,1,0:T(8,128)(2,1)S(1)}, bf16[2,6,8,1152]{3,2,1,0:T(8,128)(2,1)S(1)}, u32[]{:S(2)}, u32[]{:S(2)}) collective-permute-start(bf16[2,6,8,1152]{3,2,1,0:T(8,128)(2,1)S(1)} %get-tuple-element.235), channel_id=1, source_target_pairs={{32,0},{64,32},{96,64},{128,96},{160,128},{192,160},{224,192},{33,... | collective-permute-start | bytes 663560 | tf_op jit(solution)/shard_map/ppermute | solution.py:28
  180.7 8.2 %collective-permute-start.1 = (bf16[2,6,8,1152]{3,2,1,0:T(8,128)(2,1)S(1)}, bf16[2,6,8,1152]{3,2,1,0:T(8,128)(2,1)S(1)}, u32[]{:S(2)}, u32[]{:S(2)}) collective-permute-start(bf16[2,6,8,1152]{3,2,1,0:T(8,128)(2,1)S(1)} %get-tuple-element.234), channel_id=1, source_target_pairs={{0,32},{32,64},{64,96},{96,128},{128,160},{160,192},{192,224},{1,3... | collective-permute-start | bytes 663560 | tf_op jit(solution)/shard_map/ppermute | solution.py:25
  189.0 0.7 copy-start.4
  192.2 50.8 %collective-permute-start.4 = (bf16[2,20,6,1152]{3,0,2,1:T(2,128)(2,1)}, bf16[2,20,6,1152]{3,0,2,1:T(2,128)(2,1)}, u32[]{:S(2)}, u32[]{:S(2)}) collective-permute-start(bf16[2,20,6,1152]{3,0,2,1:T(2,128)(2,1)} %copy.69), channel_id=1, source_target_pairs={{1,0},{2,1},{3,2},{4,3},{5,4},{6,5},{7,6},{8,7},{9,8},{10,9},{11,1... | collective-permute-start | bytes 1658888 | tf_op jit(solution)/shard_map/ppermute | solution.py:28
  196.7 47.4 %collective-permute-start.3 = (bf16[2,20,6,1152]{3,0,2,1:T(2,128)(2,1)}, bf16[2,20,6,1152]{3,0,2,1:T(2,128)(2,1)}, u32[]{:S(2)}, u32[]{:S(2)}) collective-permute-start(bf16[2,20,6,1152]{3,0,2,1:T(2,128)(2,1)} %copy.68), channel_id=1, source_target_pairs={{0,1},{1,2},{2,3},{3,4},{4,5},{5,6},{6,7},{7,8},{8,9},{9,10},{10,1... | collective-permute-start | bytes 1658888 | tf_op jit(solution)/shard_map/ppermute | solution.py:25
  242.9 2.3 copy-start.5
  249.0 43.0 %collective-permute-start.5 = (bf16[2,8,8,1152]{3,2,1,0:T(8,128)(2,1)S(1)}, bf16[2,8,8,1152]{3,2,1,0:T(8,128)(2,1)}, u32[]{:S(2)}, u32[]{:S(2)}) collective-permute-start(bf16[2,8,8,1152]{3,2,1,0:T(8,128)(2,1)S(1)} %get-tuple-element.245), channel_id=1, source_target_pairs={{256,0},{257,1},{258,2},{259,3},{260,4},{261,5},{262,6},{263,7},{2... | collective-permute-start | bytes 884744 | tf_op jit(solution)/shard_map/ppermute | solution.py:36
  297.9 7.9 %collective-permute-start.7 = (bf16[2,6,8,1152]{3,2,1,0:T(8,128)(2,1)S(1)}, bf16[2,6,8,1152]{3,2,1,0:T(8,128)(2,1)S(1)}, u32[]{:S(2)}, u32[]{:S(2)}) collective-permute-start(bf16[2,6,8,1152]{3,2,1,0:T(8,128)(2,1)S(1)} %get-tuple-element.233), channel_id=1, source_target_pairs={{32,0},{64,32},{96,64},{128,96},{160,128},{192,160},{224,192},{33,... | collective-permute-start | bytes 663560 | tf_op jit(solution)/shard_map/ppermute | solution.py:28
  299.2 7.5 %collective-permute-start.6 = (bf16[2,6,8,1152]{3,2,1,0:T(8,128)(2,1)S(1)}, bf16[2,6,8,1152]{3,2,1,0:T(8,128)(2,1)S(1)}, u32[]{:S(2)}, u32[]{:S(2)}) collective-permute-start(bf16[2,6,8,1152]{3,2,1,0:T(8,128)(2,1)S(1)} %get-tuple-element.232), channel_id=1, source_target_pairs={{0,32},{32,64},{64,96},{96,128},{128,160},{160,192},{192,224},{1,3... | collective-permute-start | bytes 663560 | tf_op jit(solution)/shard_map/ppermute | solution.py:25
  308.4 24.3 %collective-permute-start.9 = (bf16[2,20,6,1152]{3,0,2,1:T(2,128)(2,1)S(1)}, bf16[2,20,6,1152]{3,0,2,1:T(2,128)(2,1)S(1)}, u32[]{:S(2)}, u32[]{:S(2)}) collective-permute-start(bf16[2,20,6,1152]{3,0,2,1:T(2,128)(2,1)S(1)} %copy.77), channel_id=1, source_target_pairs={{1,0},{2,1},{3,2},{4,3},{5,4},{6,5},{7,6},{8,7},{9,8},{10,9},{11,1... | collective-permute-start | bytes 1658888 | tf_op jit(solution)/shard_map/ppermute | solution.py:28
  312.9 19.9 %collective-permute-start.8 = (bf16[2,20,6,1152]{3,0,2,1:T(2,128)(2,1)S(1)}, bf16[2,20,6,1152]{3,0,2,1:T(2,128)(2,1)S(1)}, u32[]{:S(2)}, u32[]{:S(2)}) collective-permute-start(bf16[2,20,6,1152]{3,0,2,1:T(2,128)(2,1)S(1)} %copy.76), channel_id=1, source_target_pairs={{0,1},{1,2},{2,3},{3,4},{4,5},{5,6},{6,7},{7,8},{8,9},{9,10},{10,1... | collective-permute-start | bytes 1658888 | tf_op jit(solution)/shard_map/ppermute | solution.py:25
  332.9 3.1 copy-start.1
  336.0 8.7 %copy-start.8 = (bf16[128,576]{0,1:T(8,128)(2,1)}, bf16[128,576]{0,1:T(8,128)(2,1)S(1)}, u32[]{:S(2)}) copy-start(bf16[128,576]{0,1:T(8,128)(2,1)S(1)} %get-tuple-element.205) | copy-start | bytes 442372 | tf_op jit(solution)/shard_map/cond
  349.6 3.2 copy-start.9
  353.6 3.6 copy-start.2
Sparse Core Ops, SparseCore 0:
  9.5 84.4 all-gather.4
  96.2 70.3 all-gather.6
  168.8 68.9 all-gather.8
